TPU v7x, 32 devices: a whole 2x2x4 slice. The times are simulated.
32 devices in a mesh: dp: 4 (over x, core), seq: 8 (over z, y).
Axes of the slice: x: 2, y: 2, z: 4, core: 2. Of those that a mesh axis runs over, the one named last changes fastest.
Arguments:
- queries: bfloat16 [4, 2048, 1024], P('dp', 'seq'), may hold values from -6 to 6
- keys: bfloat16 [4, 2048, 1024], P('dp', 'seq'), may hold values from -6 to 6
- values: bfloat16 [4, 2048, 1024], P('dp', 'seq'), may hold values from -6 to 6
- out_weight: bfloat16 [1024, 1024], replicated, may hold values from -0.1875 to 0.1875
- cotangent: bfloat16 [4, 2048, 1024], P('dp', 'seq'), may hold values from -6 to 6
Outputs:
- mixed: bfloat16 [4, 2048, 1024], P('dp', 'seq')
- grad_out_weight: float32 [1024, 1024], P(('dp', 'seq'))
- grad_queries: bfloat16 [4, 2048, 1024], P('dp', 'seq')
- grad_keys: bfloat16 [4, 2048, 1024], P('dp', 'seq')
- grad_values: bfloat16 [4, 2048, 1024], P('dp', 'seq')
All inputs are finite; a program needn't handle non-finite values.
Results may differ from a plain program's by a relative error of at most 0.02.
Values may be sent and summed in bfloat16 or wider, within the bound.
A program may use at most 128 MiB of HBM per device.

v0:
```python
import functools
import math

import jax
import jax.numpy as jnp
from jax import lax
from jax.experimental import pallas as pl
from jax.experimental.pallas import tpu as pltpu
from jax.sharding import PartitionSpec as P

HEADS = 16
HEAD_DIM = 64
BLOCK = 64
MASKED = -1e30
SLOT = 16
F32 = jnp.float32
BF16 = jnp.bfloat16


def dot(a, b):
    return lax.dot_general(a, b, (((1,), (0,)), ((), ())), preferred_element_type=F32)


def dot_nt(a, b):
    return lax.dot_general(a, b, (((1,), (1,)), ((), ())), preferred_element_type=F32)


def dot_tn(a, b):
    return lax.dot_general(a, b, (((0,), (0,)), ((), ())), preferred_element_type=F32)


def iota(shape, dim):
    return lax.broadcasted_iota(jnp.int32, shape, dim)


def kernel(
    n, span_one, span_two,
    q_ref, k_ref, v_ref, w_ref, c_ref,
    mixed_ref, gw_ref, gq_ref, gk_ref, gv_ref,
    kext, vext, pool, da_ref, att_ref, bias, qx, ec, er, mcs, lcs, ncs, e_ref, inv_ref, wt_ref,
    g_ref, h_ref, gqa, dke, dve, hs, hr, dcs, dcr,
    pool_send, pool_recv, halo_send, halo_recv, back_send, back_recv, edge_send, edge_recv,
):
    rows, hidden = q_ref.shape
    blocks = rows // BLOCK
    pairs = hidden // 128
    halves = rows // 128
    widths = (BLOCK, 2 * BLOCK, 4 * BLOCK)
    scale = 1.0 / math.sqrt(HEAD_DIM)
    me = lax.axis_index("seq")
    heads = HEADS
    hr_rows = blocks * heads
    has_left, has_right = me > 0, me < n - 1

    barrier = pltpu.get_barrier_semaphore()
    for o in range(1, n):
        pl.semaphore_signal(
            barrier, inc=1, device_id={"seq": lax.rem(me + o, n)}, device_id_type=pl.DeviceIdType.MESH
        )
    pl.semaphore_wait(barrier, n - 1)

    def remote(src, dst, ssem, rsem, peer):
        return pltpu.make_async_remote_copy(
            src_ref=src, dst_ref=dst, send_sem=ssem, recv_sem=rsem,
            device_id={"seq": peer}, device_id_type=pl.DeviceIdType.MESH,
        )

    left = lax.rem(me + n - 1, n)
    right = lax.rem(me + 1, n)
    top = pl.ds(0, BLOCK)
    last = pl.ds(rows - BLOCK, BLOCK)
    bottom = pl.ds(rows + BLOCK, BLOCK)
    to_right = [
        remote(k_ref.at[last], kext.at[top], halo_send.at[0], halo_recv.at[0], right),
        remote(v_ref.at[last], vext.at[top], halo_send.at[1], halo_recv.at[1], right),
    ]
    to_left = [
        remote(k_ref.at[top], kext.at[bottom], halo_send.at[2], halo_recv.at[2], left),
        remote(v_ref.at[top], vext.at[bottom], halo_send.at[3], halo_recv.at[3], left),
    ]

    r_id, i_id = iota((SLOT, rows), 0), iota((SLOT, rows), 1)

    def pick(rid):
        base, hit = 0, jnp.zeros((SLOT, rows), jnp.bool_)
        for width in widths:
            count = rows // width
            inside = jnp.logical_and(rid >= base, rid < base + count)
            hit = jnp.logical_or(hit, jnp.logical_and(inside, i_id // width == rid - base))
            base += count
        return jnp.where(hit, 1.0, 0.0).astype(BF16)

    first1 = rows // widths[0]
    first2 = first1 + rows // widths[1]

    def row_scale(shape):
        rr = iota(shape, 0) % 8
        return jnp.where(
            rr < first1,
            1.0 / math.sqrt(widths[0]),
            jnp.where(rr < first2, 1.0 / math.sqrt(widths[1]), 1.0 / math.sqrt(widths[2])),
        )

    pooled = dot(pick(r_id), k_ref[...]) + dot(pick(r_id - 8), v_ref[...])
    pool[me] = (pooled * row_scale((SLOT, 1))).astype(BF16)

    for o in range(1, n):
        peer = lax.rem(me + o, n)
        remote(pool.at[me], pool.at[me], pool_send.at[o], pool_recv.at[o], peer).start()

    @pl.when(has_right)
    def _():
        for copy in to_right:
            copy.start()

    @pl.when(has_left)
    def _():
        for copy in to_left:
            copy.start()

    kext[BLOCK : BLOCK + rows] = k_ref[...]
    vext[BLOCK : BLOCK + rows] = v_ref[...]

    @pl.when(me == 0)
    def _():
        kext[0:BLOCK] = jnp.zeros((BLOCK, hidden), BF16)
        vext[0:BLOCK] = jnp.zeros((BLOCK, hidden), BF16)

    @pl.when(me == n - 1)
    def _():
        kext[rows + BLOCK :] = jnp.zeros((BLOCK, hidden), BF16)
        vext[rows + BLOCK :] = jnp.zeros((BLOCK, hidden), BF16)

    da_ref[...] = dot_nt(c_ref[...], w_ref[...]).astype(BF16)

    for b in range(halves):
        qb = (iota((256, 256), 0) % 128) // BLOCK + 1
        kb = iota((256, 256), 1) // BLOCK
        ok = jnp.abs(qb - kb) <= 1
        if b == 0:
            ok = jnp.logical_and(ok, jnp.logical_or(kb > 0, has_left))
        if b == halves - 1:
            ok = jnp.logical_and(ok, jnp.logical_or(kb < 3, has_right))
        bias[b] = jnp.where(ok, 0.0, MASKED)

    x_id, xi_id = iota((hr_rows, rows), 0) // heads, iota((hr_rows, rows), 1)
    head_mask = iota((hr_rows, hidden), 1) // HEAD_DIM == iota((hr_rows, hidden), 0) % heads
    for level, width in enumerate(widths):
        hit = xi_id // width == x_id * BLOCK // width
        rows_q = dot(jnp.where(hit, 1.0, 0.0).astype(BF16), q_ref[...]) * (1.0 / math.sqrt(width))
        rows_q = rows_q.astype(BF16).astype(F32) * scale
        qx[level] = jnp.where(head_mask, rows_q, 0.0).astype(BF16)

    cols = SLOT * n
    t_id = iota((hr_rows, cols), 0) // heads
    dev, rr = iota((hr_rows, cols), 1) // SLOT, iota((hr_rows, cols), 1) % SLOT
    same_one = dev // span_one == me // span_one
    same_two = dev // span_two == me // span_two
    gap = jnp.abs(me * first1 + t_id - dev * first1 - rr)
    allowed = (
        same_one & (rr < first1) & (gap > 1),
        same_two & jnp.logical_not(same_one) & (rr >= first1) & (rr < first2),
        jnp.logical_not(same_two) & (rr >= first2) & (rr < first2 + rows // widths[2]),
    )

    for o in range(1, n):
        src = lax.rem(me + n - o, n)
        remote(pool.at[src], pool.at[src], pool_send.at[o], pool_recv.at[o], src).wait_recv()
    coarse = pool[...].reshape(cols, hidden)
    s = jnp.full((hr_rows, cols), MASKED, F32)
    for level in range(3):
        s = jnp.where(allowed[level], dot_nt(qx[level], coarse), s)
    mc = jnp.max(s, axis=1, keepdims=True)
    ex = jnp.where(s > 0.5 * MASKED, jnp.exp(s - mc), 0.0)
    ec[...] = ex
    rolled = pltpu.roll(ex, 8, 1).astype(BF16)
    er[...] = rolled
    mcs[...] = jnp.broadcast_to(mc, (hr_rows, 128))
    lcs[...] = jnp.broadcast_to(jnp.sum(ex, axis=1, keepdims=True), (hr_rows, 128))

    def fold_heads(x):
        x = jnp.where(head_mask, x, 0.0)
        return [jnp.sum(x[t * heads : (t + 1) * heads], axis=0, keepdims=True) for t in range(blocks)]

    for t, row in enumerate(fold_heads(dot(rolled, coarse))):
        ncs[t : t + 1, :] = row

    @pl.when(has_left)
    def _():
        for copy in to_right:
            copy.wait_recv()

    @pl.when(has_right)
    def _():
        for copy in to_left:
            copy.wait_recv()

    low = iota((128, 128), 1) < HEAD_DIM

    def stack(x):
        zero = jnp.zeros_like(x)
        return jnp.concatenate([jnp.where(low, x, zero), jnp.where(low, zero, x)], axis=0)

    def choose(x):
        return jnp.where(low, x[:128], x[128:])

    def forward(p, carry):
        lanes = pl.ds(pl.multiple_of(p * 128, 128), 128)
        for b in range(halves):
            u = p * halves + b
            mine, win = pl.ds(128 * b, 128), pl.ds(128 * b, 256)
            q2 = stack(q_ref[mine, lanes] * scale)
            s = dot_nt(q2, kext[win, lanes]) + bias[b]

            def per_row(ref):
                parts = []
                for h in range(2):
                    for t in (2 * b, 2 * b + 1):
                        row = ref[pl.ds(t * heads + 2 * p + h, 1), :]
                        parts.append(jnp.broadcast_to(row, (BLOCK, 128)))
                return jnp.concatenate(parts, axis=0)

            mcr = per_row(mcs)
            m = jnp.maximum(jnp.max(s, axis=1, keepdims=True), mcr)
            e = jnp.exp(s - jnp.concatenate([m, m], axis=1))
            f = jnp.exp(mcr - m)
            inv = 1.0 / (jnp.sum(e, axis=1, keepdims=True) + per_row(lcs) * f)
            nc = jnp.concatenate(
                [jnp.broadcast_to(ncs[2 * b + t : 2 * b + t + 1, lanes], (BLOCK, 128)) for t in (0, 1, 0, 1)],
                axis=0,
            )
            num = dot(e.astype(BF16), vext[win, lanes]) + nc * f
            att_ref[mine, lanes] = choose(num * inv).astype(BF16)
            e_ref[u] = e
            inv_ref[u] = inv
            wt_ref[u] = f * inv
        return carry

    lax.fori_loop(0, pairs, forward, 0)

    mixed_ref[...] = dot(att_ref[...], w_ref[...]).astype(BF16)
    gw_ref[...] = dot_tn(att_ref[...], c_ref[...])

    dke[...] = jnp.zeros_like(dke)
    dve[...] = jnp.zeros_like(dve)

    def backward(p, carry):
        lanes = pl.ds(pl.multiple_of(p * 128, 128), 128)
        for b in range(halves):
            u = p * halves + b
            mine, win = pl.ds(128 * b, 128), pl.ds(128 * b, 256)
            q2 = stack(q_ref[mine, lanes] * scale)
            d2 = stack(da_ref[mine, lanes])
            att = att_ref[mine, lanes].astype(F32)
            d2f = d2.astype(F32)
            prod = d2f * jnp.concatenate([att, att], axis=0)
            delta = jnp.sum(prod, axis=1, keepdims=True)
            inv = inv_ref[u]
            pr = e_ref[u] * jnp.concatenate([inv, inv], axis=1)
            kw = kext[win, lanes]
            ds = (pr * (dot_nt(d2, vext[win, lanes]) - delta)).astype(BF16)
            gqa[mine, lanes] = choose(dot(ds, kw)) * scale
            dke[win, lanes] += dot_tn(ds, q2)
            dve[win, lanes] += dot_tn(pr.astype(BF16), d2)
            wt = wt_ref[u]
            for ref, x in ((g_ref, wt * d2f), (h_ref, wt * prod)):
                x = x[:128] + x[128:]
                for t in range(2):
                    ref[2 * b + t : 2 * b + t + 1, lanes] = jnp.sum(
                        x[t * BLOCK : (t + 1) * BLOCK], axis=0, keepdims=True
                    )
        return carry

    lax.fori_loop(0, pairs, backward, 0)

    hs[0] = dke[rows + BLOCK :].astype(BF16)
    hs[1] = dve[rows + BLOCK :].astype(BF16)
    hs[2] = dke[0:BLOCK].astype(BF16)
    hs[3] = dve[0:BLOCK].astype(BF16)
    edge_right = [remote(hs.at[i], hr.at[i], edge_send.at[i], edge_recv.at[i], right) for i in (0, 1)]
    edge_left = [remote(hs.at[i], hr.at[i], edge_send.at[i], edge_recv.at[i], left) for i in (2, 3)]

    @pl.when(has_right)
    def _():
        for copy in edge_right:
            copy.start()

    @pl.when(has_left)
    def _():
        for copy in edge_left:
            copy.start()

    def spread(ref):
        x = jnp.concatenate(
            [jnp.broadcast_to(ref[t : t + 1, :], (heads, hidden)) for t in range(blocks)], axis=0
        )
        return jnp.where(head_mask, x, 0.0)

    gx = spread(g_ref).astype(BF16)
    hsum = jnp.sum(spread(h_ref), axis=1, keepdims=True)
    ds = ec[...] * (pltpu.roll(dot_nt(gx, coarse), cols - 8, 1) - hsum)
    grad = dot_tn(er[...], gx)
    mix = jnp.zeros((hr_rows, cols), F32)
    a_id, b_id = iota((hr_rows, hr_rows), 0), iota((hr_rows, hr_rows), 1)
    for level, width in enumerate(widths):
        dsl = jnp.where(allowed[level], ds, 0.0).astype(BF16)
        grad = grad + dot_tn(dsl, qx[level])
        span = width // BLOCK * heads
        same = (a_id // span == b_id // span) & (a_id % heads == b_id % heads)
        mix = mix + dot(jnp.where(same, 1.0, 0.0).astype(BF16), dsl) * (scale / math.sqrt(width))
    dcs[...] = grad.astype(BF16).reshape(n, SLOT, hidden)
    for o in range(1, n):
        peer = lax.rem(me + o, n)
        remote(dcs.at[peer], dcr.at[o], back_send.at[o], back_recv.at[o], peer).start()

    for t, row in enumerate(fold_heads(dot(mix.astype(BF16), coarse))):
        part = pl.ds(t * BLOCK, BLOCK)
        gq_ref[part, :] = (gqa[part, :] + row).astype(BF16)

    total = dcs[me].astype(F32)
    for o in range(1, n):
        src = lax.rem(me + n - o, n)
        remote(dcs.at[src], dcr.at[o], back_send.at[o], back_recv.at[o], src).wait_recv()
        total = total + dcr[o].astype(F32)
    total = total * row_scale((SLOT, 1))

    @pl.when(has_left)
    def _():
        for i, acc in ((0, dke), (1, dve)):
            edge_right[i].wait_recv()
            acc[BLOCK : 2 * BLOCK] += hr[i].astype(F32)

    @pl.when(has_right)
    def _():
        for i, acc in ((0, dke), (1, dve)):
            edge_left[i].wait_recv()
            acc[rows : rows + BLOCK] += hr[2 + i].astype(F32)

    for t in range(blocks):
        part = pl.ds(t * BLOCK, BLOCK)
        for base, acc, out in ((0, dke, gk_ref), (8, dve, gv_ref)):
            row = total[base + t : base + t + 1]
            second = base + first1 + t // 2
            third = base + first2 + t // 4
            row = row + total[second : second + 1] + total[third : third + 1]
            out[part, :] = (acc[pl.ds((t + 1) * BLOCK, BLOCK), :] + row).astype(BF16)

    for o in range(1, n):
        peer = lax.rem(me + o, n)
        remote(pool.at[me], pool.at[me], pool_send.at[o], pool_recv.at[o], peer).wait_send()
        remote(dcs.at[peer], dcr.at[o], back_send.at[o], back_recv.at[o], peer).wait_send()

    @pl.when(has_right)
    def _():
        for copy in to_right + edge_right:
            copy.wait_send()

    @pl.when(has_left)
    def _():
        for copy in to_left + edge_left:
            copy.wait_send()


def on_device(queries, keys, values, out_weight, cotangent):
    n = lax.axis_size("seq")
    rows, hidden = queries.shape[1:]
    span_one, span_two = max(2, n // 8), n // 2
    units = (hidden // 128) * (rows // 128)
    hrows = rows // BLOCK * HEADS
    ext = rows + 2 * BLOCK
    vm = pl.BlockSpec(memory_space=pltpu.VMEM)
    act = jax.ShapeDtypeStruct((rows, hidden), BF16)
    dma = pltpu.SemaphoreType.DMA
    mixed, gw, gq, gk, gv = pl.pallas_call(
        functools.partial(kernel, n, span_one, span_two),
        out_shape=(act, jax.ShapeDtypeStruct((hidden, hidden), F32), act, act, act),
        in_specs=[vm] * 5,
        out_specs=(vm,) * 5,
        scratch_shapes=[
            pltpu.VMEM((ext, hidden), BF16),
            pltpu.VMEM((ext, hidden), BF16),
            pltpu.VMEM((n, SLOT, hidden), BF16),
            pltpu.VMEM((rows, hidden), BF16),
            pltpu.VMEM((rows, hidden), BF16),
            pltpu.VMEM((rows // 128, 256, 256), F32),
            pltpu.VMEM((3, hrows, hidden), BF16),
            pltpu.VMEM((hrows, SLOT * n), F32),
            pltpu.VMEM((hrows, SLOT * n), BF16),
            pltpu.VMEM((hrows, 128), F32),
            pltpu.VMEM((hrows, 128), F32),
            pltpu.VMEM((8, hidden), F32),
            pltpu.VMEM((units, 256, 256), F32),
            pltpu.VMEM((units, 256, 128), F32),
            pltpu.VMEM((units, 256, 128), F32),
            pltpu.VMEM((8, hidden), F32),
            pltpu.VMEM((8, hidden), F32),
            pltpu.VMEM((rows, hidden), F32),
            pltpu.VMEM((ext, hidden), F32),
            pltpu.VMEM((ext, hidden), F32),
            pltpu.VMEM((4, BLOCK, hidden), BF16),
            pltpu.VMEM((4, BLOCK, hidden), BF16),
            pltpu.VMEM((n, SLOT, hidden), BF16),
            pltpu.VMEM((n, SLOT, hidden), BF16),
            dma((n,)), dma((n,)), dma((4,)), dma((4,)), dma((n,)), dma((n,)), dma((4,)), dma((4,)),
        ],
        compiler_params=pltpu.CompilerParams(
            collective_id=0, has_side_effects=True, vmem_limit_bytes=56 * 1024 * 1024
        ),
    )(queries[0], keys[0], values[0], out_weight, cotangent[0])
    gw = lax.psum_scatter(gw, ("dp", "seq"), scatter_dimension=0, tiled=True)
    return mixed[None], gw, gq[None], gk[None], gv[None]


def solution(mesh):
    tokens = P("dp", "seq", None)
    return jax.shard_map(
        on_device,
        mesh=mesh,
        in_specs=(tokens, tokens, tokens, P(), tokens),
        out_specs=(tokens, P(("dp", "seq"), None), tokens, tokens, tokens),
        check_vma=False,
    )
```

profile of v0, /device:TPU:0, one launch (start us, length us, event | category | flops | bytes accessed | tf_op | source)
XLA Modules:
  0.0 214.3 jit_solution(15706339741427831026)
XLA Ops:
  7.2 0.0 reduce-scatter.2.cloned.1.call-start
  7.2 50.9 %shard_map.92 = (bf16[256,1024]{1,0:T(8,128)(2,1)}, f32[1024,1024]{1,0:T(8,128)}, bf16[256,1024]{1,0:T(8,128)(2,1)}, bf16[256,1024]{1,0:T(8,128)(2,1)}, bf16[256,1024]{1,0:T(8,128)(2,1)}) custom-call(bf16[256,1024]{1,0:T(8,128)(2,1)} %bitcast.12, bf16[256,1024]{1,0:T(8,128)(2,1)} %bitcast.13, bf16[256,1024]{1,0:T(8,128)(2,1)} %bitcast.14, ...), custom_call_target="tpu_custom_call" | custom-call | tf_op jit(solution)/shard_map/pallas_call | solution.py:374
  58.1 0.0 copy-start.3
  58.1 0.0 copy-start.2
  58.1 0.0 copy-start.1
  58.1 0.0 copy-start
  58.1 0.0 reduce-scatter.2.cloned.1.call-update
  58.2 146.1 %reduce-scatter.2.cloned.1.call-done = f32[32,1024]{1,0:T(8,128)} async-done(((f32[1024,1024]{1,0:T(8,128)}), f32[32,1024]{1,0:T(8,128)}) %reduce-scatter.2.cloned.1.call-update) | async-done | bytes 131088 | tf_op jit(solution)/shard_map/reduce_scatter | solution.py:410
  204.3 0.0 copy-done.3
  204.3 0.8 copy.14
  205.1 0.0 copy-done.2
  205.1 0.8 copy.15
  205.9 0.0 copy-done.1
  205.9 0.8 copy.16
  206.7 0.0 copy-done
  206.7 0.8 copy.17
Async XLA Ops:
  7.2 197.1 %reduce-scatter.2.cloned.1.call-start = ((), (), s32[]{:S(2)}) async-start(), calls=%async_computation.1 | async-start | bytes 4325376 | tf_op jit(solution)/shard_map/reduce_scatter | solution.py:410
  58.1 146.2 %copy-start.3 = (bf16[256,1024]{1,0:T(8,128)(2,1)S(1)}, bf16[256,1024]{1,0:T(8,128)(2,1)}, u32[]{:S(2)}) copy-start(bf16[256,1024]{1,0:T(8,128)(2,1)} %get-tuple-element.10) | copy-start | bytes 1572868
  58.1 147.0 %copy-start.2 = (bf16[256,1024]{1,0:T(8,128)(2,1)S(1)}, bf16[256,1024]{1,0:T(8,128)(2,1)}, u32[]{:S(2)}) copy-start(bf16[256,1024]{1,0:T(8,128)(2,1)} %get-tuple-element.12) | copy-start | bytes 1572868
  58.1 147.8 %copy-start.1 = (bf16[256,1024]{1,0:T(8,128)(2,1)S(1)}, bf16[256,1024]{1,0:T(8,128)(2,1)}, u32[]{:S(2)}) copy-start(bf16[256,1024]{1,0:T(8,128)(2,1)} %get-tuple-element.13) | copy-start | bytes 1572868
  58.1 148.6 %copy-start = (bf16[256,1024]{1,0:T(8,128)(2,1)S(1)}, bf16[256,1024]{1,0:T(8,128)(2,1)}, u32[]{:S(2)}) copy-start(bf16[256,1024]{1,0:T(8,128)(2,1)} %get-tuple-element.14) | copy-start | bytes 1572868
Sparse Core Ops, SparseCore 0:
  58.3 145.9 reduce-scatter.1
where the time goes:
time: 214 us
  waiting for transfers between devices  146 us (68%)
  Pallas kernels  50.9 us (24%)
  between operations  14.1 us (7%)
  local copies, waits for them, and re-layouts  3.19 us (1%)
    reduce_scatter x1, waiting for transfers between devices, on_device(): gw = lax.psum_scatter(gw, ('dp', 'seq'), scatter_dimension=0, tiled=True)  146 us
    pallas_call x1, Pallas kernels, on_device(): pl.pallas_call(functools.partial(kernel, n, span_one, span_two), out_shap...  50.9 us
  transfers between devices with their start and end apart: 1, of which 1 were waited for; matrix products, arithmetic and copies ran while one was open for 0% of the time, Pallas kernels for 0%

commit v1 on v0

--- a/solution.py
+++ b/solution.py
@@ -39,7 +39,9 @@
     mixed_ref, gw_ref, gq_ref, gk_ref, gv_ref,
     kext, vext, pool, da_ref, att_ref, bias, qx, ec, er, mcs, lcs, ncs, e_ref, inv_ref, wt_ref,
     g_ref, h_ref, gqa, dke, dve, hs, hr, dcs, dcr,
+    gwb, ra, s1, r1, k1, s2, r2, k2, sd, rd,
     pool_send, pool_recv, halo_send, halo_recv, back_send, back_recv, edge_send, edge_recv,
+    tree_send, tree_recv, ring_send, ring_recv,
 ):
     rows, hidden = q_ref.shape
     blocks = rows // BLOCK
@@ -57,13 +59,116 @@
         pl.semaphore_signal(
             barrier, inc=1, device_id={"seq": lax.rem(me + o, n)}, device_id_type=pl.DeviceIdType.MESH
         )
-    pl.semaphore_wait(barrier, n - 1)
-
-    def remote(src, dst, ssem, rsem, peer):
+    dp = lax.axis_index("dp")
+    core, side = dp % 2, dp // 2
+    mate, across = dp + 1 - 2 * core, lax.rem(dp + 2, 4)
+    for peer in (mate, across):
+        pl.semaphore_signal(
+            barrier, inc=1, device_id={"dp": peer}, device_id_type=pl.DeviceIdType.MESH
+        )
+    pl.semaphore_wait(barrier, n + 1)
+
+    def remote(src, dst, ssem, rsem, peer, axis="seq"):
         return pltpu.make_async_remote_copy(
             src_ref=src, dst_ref=dst, send_sem=ssem, recv_sem=rsem,
-            device_id={"seq": peer}, device_id_type=pl.DeviceIdType.MESH,
-        )
+            device_id={axis: peer}, device_id_type=pl.DeviceIdType.MESH,
+        )
+
+    own = hidden // 4
+    half = hidden // 2
+    parity, place = me % 2, me // 2
+    twin = me + 1 - 2 * parity
+    groups = n // 2
+    part_rows = own // n
+
+    def tree(i, src, dst, axis):
+        peer = {"core": mate, "x": across, "y": twin}[axis]
+        return remote(src, dst, tree_send.at[i], tree_recv.at[i], peer, "seq" if axis == "y" else "dp")
+
+    first_hop = [tree(i, gwb.at[i, 1 - core], ra.at[i], "core") for i in (0, 1)]
+    second_hop = [tree(2 + i, s1.at[i], r1.at[i], "xy"[i]) for i in (0, 1)]
+    third_hop = [tree(4 + i, s2.at[i], r2.at[i], "yx"[i]) for i in (0, 1)]
+
+    def by_parity(x):
+        low = jnp.concatenate(
+            [x[2 * j * part_rows : (2 * j + 1) * part_rows] for j in range(groups)], axis=0
+        )
+        high = jnp.concatenate(
+            [x[(2 * j + 1) * part_rows : (2 * j + 2) * part_rows] for j in range(groups)], axis=0
+        )
+        return jnp.where(parity == 1, high, low), jnp.where(parity == 1, low, high)
+
+    def by_side(low, high):
+        return jnp.where(side == 1, high, low), jnp.where(side == 1, low, high)
+
+    def partial_products(c):
+        for x in range(2):
+            columns = pl.ds(pl.multiple_of((2 * x + c) * own, own), own)
+            y = dot_tn(att_ref[:, columns], c_ref[...]).astype(BF16)
+            gwb[0, c, x] = y[:, :half]
+            gwb[1, c, x] = y[:, half:]
+
+    def start_first():
+        partial_products(1 - core)
+        for copy in first_hop:
+            copy.start()
+        partial_products(core)
+
+    def start_second():
+        for i in (0, 1):
+            first_hop[i].wait_recv()
+            low, high = [gwb[i, core, x].astype(F32) + ra[i, x].astype(F32) for x in range(2)]
+            if i == 0:
+                keep, send = by_side(low, high)
+            else:
+                keep_low, send_low = by_parity(low)
+                keep_high, send_high = by_parity(high)
+                keep = jnp.concatenate([keep_low, keep_high], axis=0)
+                send = jnp.concatenate([send_low, send_high], axis=0)
+            k1[i] = keep
+            s1[i] = send.astype(BF16)
+            second_hop[i].start()
+
+    def start_third():
+        for i in (0, 1):
+            second_hop[i].wait_recv()
+            x = k1[i] + r1[i].astype(F32)
+            keep, send = by_parity(x) if i == 0 else by_side(x[: own // 2], x[own // 2 :])
+            k2[i] = keep
+            s2[i] = send.astype(BF16)
+            third_hop[i].start()
+
+    def last_hop(o, slot, peer):
+        return remote(sd.at[slot], rd.at[o], ring_send.at[o], ring_recv.at[o], 2 * peer + parity)
+
+    def start_last():
+        for i in (0, 1):
+            third_hop[i].wait_recv()
+            x = k2[i] + r2[i].astype(F32)
+            k2[i] = x
+            for j in range(groups):
+                sd[j, i * part_rows : (i + 1) * part_rows] = x[
+                    j * part_rows : (j + 1) * part_rows
+                ].astype(BF16)
+        for o in range(1, groups):
+            peer = lax.rem(place + o, groups)
+            last_hop(o, peer, peer).start()
+
+    def finish_weight():
+        mine = pl.ds(pl.multiple_of(place * part_rows, part_rows), part_rows)
+        totals = [k2[i, mine] for i in (0, 1)]
+        for o in range(1, groups):
+            src = lax.rem(place + groups - o, groups)
+            last_hop(o, src, src).wait_recv()
+            x = rd[o].astype(F32)
+            totals = [totals[0] + x[:part_rows], totals[1] + x[part_rows:]]
+        gw_ref[:, :half] = totals[0]
+        gw_ref[:, half:] = totals[1]
+        for o in range(1, groups):
+            peer = lax.rem(place + o, groups)
+            last_hop(o, peer, peer).wait_send()
+        for copy in first_hop + second_hop + third_hop:
+            copy.wait_send()
 
     left = lax.rem(me + n - 1, n)
     right = lax.rem(me + 1, n)
@@ -238,8 +343,8 @@
 
     lax.fori_loop(0, pairs, forward, 0)
 
+    start_first()
     mixed_ref[...] = dot(att_ref[...], w_ref[...]).astype(BF16)
-    gw_ref[...] = dot_tn(att_ref[...], c_ref[...])
 
     dke[...] = jnp.zeros_like(dke)
     dve[...] = jnp.zeros_like(dve)
@@ -271,7 +376,9 @@
                     )
         return carry
 
-    lax.fori_loop(0, pairs, backward, 0)
+    lax.fori_loop(0, pairs // 4, backward, 0)
+    start_second()
+    lax.fori_loop(pairs // 4, pairs, backward, 0)
 
     hs[0] = dke[rows + BLOCK :].astype(BF16)
     hs[1] = dve[rows + BLOCK :].astype(BF16)
@@ -289,6 +396,8 @@
     def _():
         for copy in edge_left:
             copy.start()
+
+    start_third()
 
     def spread(ref):
         x = jnp.concatenate(
@@ -317,6 +426,7 @@
         part = pl.ds(t * BLOCK, BLOCK)
         gq_ref[part, :] = (gqa[part, :] + row).astype(BF16)
 
+    start_last()
     total = dcs[me].astype(F32)
     for o in range(1, n):
         src = lax.rem(me + n - o, n)
@@ -345,6 +455,7 @@
             row = row + total[second : second + 1] + total[third : third + 1]
             out[part, :] = (acc[pl.ds((t + 1) * BLOCK, BLOCK), :] + row).astype(BF16)
 
+    finish_weight()
     for o in range(1, n):
         peer = lax.rem(me + o, n)
         remote(pool.at[me], pool.at[me], pool_send.at[o], pool_recv.at[o], peer).wait_send()
@@ -369,11 +480,12 @@
     hrows = rows // BLOCK * HEADS
     ext = rows + 2 * BLOCK
     vm = pl.BlockSpec(memory_space=pltpu.VMEM)
+    own, half = hidden // 4, hidden // 2
     act = jax.ShapeDtypeStruct((rows, hidden), BF16)
     dma = pltpu.SemaphoreType.DMA
     mixed, gw, gq, gk, gv = pl.pallas_call(
         functools.partial(kernel, n, span_one, span_two),
-        out_shape=(act, jax.ShapeDtypeStruct((hidden, hidden), F32), act, act, act),
+        out_shape=(act, jax.ShapeDtypeStruct((own // n, hidden), F32), act, act, act),
         in_specs=[vm] * 5,
         out_specs=(vm,) * 5,
         scratch_shapes=[
@@ -401,13 +513,23 @@
             pltpu.VMEM((4, BLOCK, hidden), BF16),
             pltpu.VMEM((n, SLOT, hidden), BF16),
             pltpu.VMEM((n, SLOT, hidden), BF16),
+            pltpu.VMEM((2, 2, 2, own, half), BF16),
+            pltpu.VMEM((2, 2, own, half), BF16),
+            pltpu.VMEM((2, own, half), BF16),
+            pltpu.VMEM((2, own, half), BF16),
+            pltpu.VMEM((2, own, half), F32),
+            pltpu.VMEM((2, own // 2, half), BF16),
+            pltpu.VMEM((2, own // 2, half), BF16),
+            pltpu.VMEM((2, own // 2, half), F32),
+            pltpu.VMEM((n // 2, 2 * own // n, half), BF16),
+            pltpu.VMEM((n // 2, 2 * own // n, half), BF16),
             dma((n,)), dma((n,)), dma((4,)), dma((4,)), dma((n,)), dma((n,)), dma((4,)), dma((4,)),
+            dma((6,)), dma((6,)), dma((n // 2,)), dma((n // 2,)),
         ],
         compiler_params=pltpu.CompilerParams(
             collective_id=0, has_side_effects=True, vmem_limit_bytes=56 * 1024 * 1024
         ),
     )(queries[0], keys[0], values[0], out_weight, cotangent[0])
-    gw = lax.psum_scatter(gw, ("dp", "seq"), scatter_dimension=0, tiled=True)
     return mixed[None], gw, gq[None], gk[None], gv[None]
 
 

time: 214 us -> 70.3 us (0.33)
  waiting for transfers between devices: 146 us -> 0 us
  between operations: 14.1 us -> 0.66 us
  Pallas kernels: 50.9 us -> 62.4 us
  local copies, waits for them, and re-layouts: 3.19 us -> 6.98 us
    reduce_scatter x1 -> x0, waiting for transfers between devices: 146 us -> none  [on_device(): gw = lax.psum_scatter(gw, ('dp', 'seq'), scatter_dimension=0, tiled=True)]
    pallas_call x1, Pallas kernels: 50.9 us -> 62.4 us  [on_device(): pl.pallas_call(functools.partial(kernel, n, span_one, span_two), out_shap...]
    unnamed x12 -> x9, local copies, waits for them, and re-layouts: 3.19 us -> 6.98 us
  transfers between devices with their start and end apart: 1 -> 0, of which waited for: 1 -> 0; matrix products, arithmetic and copies ran while one was open for 0% -> 0% of each run, Pallas kernels for 0% -> 0%
where the time goes in v1:
time: 70.3 us; the launch traced here: 70.1 us
  Pallas kernels  62.4 us (89%)
  local copies, waits for them, and re-layouts  6.98 us (10%)
    pallas_call x1, Pallas kernels, on_device(): pl.pallas_call(functools.partial(kernel, n, span_one, span_two), out_shap...  62.4 us
    unnamed x9, local copies, waits for them, and re-layouts  6.98 us

profile of v1, /device:TPU:0, one launch (start us, length us, event | category | flops | bytes accessed | tf_op | source)
XLA Modules:
  0.0 70.1 jit_solution(16638370999755919326)
XLA Ops:
  0.6 62.4 %shard_map.92 = (bf16[256,1024]{1,0:T(8,128)(2,1)}, f32[32,1024]{1,0:T(8,128)}, bf16[256,1024]{1,0:T(8,128)(2,1)}, bf16[256,1024]{1,0:T(8,128)(2,1)}, bf16[256,1024]{1,0:T(8,128)(2,1)}) custom-call(bf16[256,1024]{1,0:T(8,128)(2,1)} %bitcast.12, bf16[256,1024]{1,0:T(8,128)(2,1)} %bitcast.13, bf16[256,1024]{1,0:T(8,128)(2,1)} %bitcast.14, ...), custom_call_target="tpu_custom_call" | custom-call | tf_op jit(solution)/shard_map/pallas_call | solution.py:486
  63.1 0.0 copy-start.1
  63.1 0.0 copy-start
  63.1 2.0 %copy.15 = bf16[1,256,1024]{2,1,0:T(8,128)(2,1)} copy(bf16[1,256,1024]{2,1,0:T(8,128)(2,1)} %bitcast.11) | data formatting | bytes 1048576
  65.0 1.6 %copy.16 = f32[32,1024]{1,0:T(8,128)} copy(f32[32,1024]{1,0:T(8,128)} %get-tuple-element.21) | data formatting | bytes 262144
  66.6 1.9 %copy.17 = bf16[1,256,1024]{2,1,0:T(8,128)(2,1)} copy(bf16[1,256,1024]{2,1,0:T(8,128)(2,1)} %bitcast.10) | data formatting | bytes 1048576
  68.5 0.0 copy-done.1
  68.5 0.8 %copy.18 = bf16[1,256,1024]{2,1,0:T(8,128)(2,1)} copy(bf16[1,256,1024]{2,1,0:T(8,128)(2,1)S(1)} %bitcast.9) | data formatting | bytes 1048576
  69.3 0.0 copy-done
  69.3 0.8 %copy.19 = bf16[1,256,1024]{2,1,0:T(8,128)(2,1)} copy(bf16[1,256,1024]{2,1,0:T(8,128)(2,1)S(1)} %bitcast.8) | data formatting | bytes 1048576
Async XLA Ops:
  63.1 5.4 %copy-start.1 = (bf16[256,1024]{1,0:T(8,128)(2,1)S(1)}, bf16[256,1024]{1,0:T(8,128)(2,1)}, u32[]{:S(2)}) copy-start(bf16[256,1024]{1,0:T(8,128)(2,1)} %get-tuple-element.13) | copy-start | bytes 1572868
  63.1 6.2 %copy-start = (bf16[256,1024]{1,0:T(8,128)(2,1)S(1)}, bf16[256,1024]{1,0:T(8,128)(2,1)}, u32[]{:S(2)}) copy-start(bf16[256,1024]{1,0:T(8,128)(2,1)} %get-tuple-element.14) | copy-start | bytes 1572868

commit v2 on v1

--- a/solution.py
+++ b/solution.py
@@ -309,7 +309,7 @@
     def choose(x):
         return jnp.where(low, x[:128], x[128:])
 
-    def forward(p, carry):
+    def forward(p):
         lanes = pl.ds(pl.multiple_of(p * 128, 128), 128)
         for b in range(halves):
             u = p * halves + b
@@ -339,18 +339,23 @@
             e_ref[u] = e
             inv_ref[u] = inv
             wt_ref[u] = f * inv
-        return carry
-
-    lax.fori_loop(0, pairs, forward, 0)
+
+    def in_twos(step, first, stop):
+        def body(i, carry):
+            step(2 * i)
+            step(2 * i + 1)
+            return carry
+
+        lax.fori_loop(first // 2, stop // 2, body, 0)
+
+    in_twos(forward, 0, pairs)
 
     start_first()
     mixed_ref[...] = dot(att_ref[...], w_ref[...]).astype(BF16)
 
-    dke[...] = jnp.zeros_like(dke)
-    dve[...] = jnp.zeros_like(dve)
-
-    def backward(p, carry):
+    def backward(p):
         lanes = pl.ds(pl.multiple_of(p * 128, 128), 128)
+        carried = None
         for b in range(halves):
             u = p * halves + b
             mine, win = pl.ds(128 * b, 128), pl.ds(128 * b, 256)
@@ -365,8 +370,13 @@
             kw = kext[win, lanes]
             ds = (pr * (dot_nt(d2, vext[win, lanes]) - delta)).astype(BF16)
             gqa[mine, lanes] = choose(dot(ds, kw)) * scale
-            dke[win, lanes] += dot_tn(ds, q2)
-            dve[win, lanes] += dot_tn(pr.astype(BF16), d2)
+            grads = [dot_tn(ds, q2), dot_tn(pr.astype(BF16), d2)]
+            for i, acc in enumerate((dke, dve)):
+                head = grads[i][:128] if b == 0 else grads[i][:128] + carried[i]
+                acc[mine, lanes] = head
+                if b == halves - 1:
+                    acc[pl.ds(128 * (b + 1), 128), lanes] = grads[i][128:]
+            carried = [x[128:] for x in grads]
             wt = wt_ref[u]
             for ref, x in ((g_ref, wt * d2f), (h_ref, wt * prod)):
                 x = x[:128] + x[128:]
@@ -374,11 +384,12 @@
                     ref[2 * b + t : 2 * b + t + 1, lanes] = jnp.sum(
                         x[t * BLOCK : (t + 1) * BLOCK], axis=0, keepdims=True
                     )
-        return carry
-
-    lax.fori_loop(0, pairs // 4, backward, 0)
+
+    in_twos(backward, 0, pairs // 4)
     start_second()
-    lax.fori_loop(pairs // 4, pairs, backward, 0)
+    in_twos(backward, pairs // 4, 3 * pairs // 4)
+    start_third()
+    in_twos(backward, 3 * pairs // 4, pairs)
 
     hs[0] = dke[rows + BLOCK :].astype(BF16)
     hs[1] = dve[rows + BLOCK :].astype(BF16)
@@ -397,7 +408,7 @@
         for copy in edge_left:
             copy.start()
 
-    start_third()
+    start_last()
 
     def spread(ref):
         x = jnp.concatenate(
@@ -426,7 +437,6 @@
         part = pl.ds(t * BLOCK, BLOCK)
         gq_ref[part, :] = (gqa[part, :] + row).astype(BF16)
 
-    start_last()
     total = dcs[me].astype(F32)
     for o in range(1, n):
         src = lax.rem(me + n - o, n)

time: 70.3 us -> 66.8 us (0.950)
  Pallas kernels: 62.4 us -> 58.9 us
    pallas_call x1, Pallas kernels: 62.4 us -> 58.9 us  [on_device(): pl.pallas_call(functools.partial(kernel, n, span_one, span_two), out_shap...]
where the time goes in v2:
time: 66.8 us; the launch traced here: 66.6 us
  Pallas kernels  58.9 us (88%)
  local copies, waits for them, and re-layouts  6.98 us (10%)
    pallas_call x1, Pallas kernels, on_device(): pl.pallas_call(functools.partial(kernel, n, span_one, span_two), out_shap...  58.9 us
    unnamed x9, local copies, waits for them, and re-layouts  6.98 us

profile of v2, /device:TPU:0, one launch (start us, length us, event | category | flops | bytes accessed | tf_op | source)
XLA Modules:
  0.0 66.6 jit_solution(690595592545523859)
XLA Ops:
  0.6 58.9 %shard_map.92 = (bf16[256,1024]{1,0:T(8,128)(2,1)}, f32[32,1024]{1,0:T(8,128)}, bf16[256,1024]{1,0:T(8,128)(2,1)}, bf16[256,1024]{1,0:T(8,128)(2,1)}, bf16[256,1024]{1,0:T(8,128)(2,1)}) custom-call(bf16[256,1024]{1,0:T(8,128)(2,1)} %bitcast.12, bf16[256,1024]{1,0:T(8,128)(2,1)} %bitcast.13, bf16[256,1024]{1,0:T(8,128)(2,1)} %bitcast.14, ...), custom_call_target="tpu_custom_call" | custom-call | tf_op jit(solution)/shard_map/pallas_call | solution.py:496
  59.6 0.0 copy-start.1
  59.6 0.0 copy-start
  59.6 2.0 %copy.15 = bf16[1,256,1024]{2,1,0:T(8,128)(2,1)} copy(bf16[1,256,1024]{2,1,0:T(8,128)(2,1)} %bitcast.11) | data formatting | bytes 1048576
  61.6 1.6 %copy.16 = f32[32,1024]{1,0:T(8,128)} copy(f32[32,1024]{1,0:T(8,128)} %get-tuple-element.21) | data formatting | bytes 262144
  63.1 1.9 %copy.17 = bf16[1,256,1024]{2,1,0:T(8,128)(2,1)} copy(bf16[1,256,1024]{2,1,0:T(8,128)(2,1)} %bitcast.10) | data formatting | bytes 1048576
  65.0 0.0 copy-done.1
  65.0 0.8 %copy.18 = bf16[1,256,1024]{2,1,0:T(8,128)(2,1)} copy(bf16[1,256,1024]{2,1,0:T(8,128)(2,1)S(1)} %bitcast.9) | data formatting | bytes 1048576
  65.8 0.0 copy-done
  65.8 0.8 %copy.19 = bf16[1,256,1024]{2,1,0:T(8,128)(2,1)} copy(bf16[1,256,1024]{2,1,0:T(8,128)(2,1)S(1)} %bitcast.8) | data formatting | bytes 1048576
Async XLA Ops:
  59.6 5.4 %copy-start.1 = (bf16[256,1024]{1,0:T(8,128)(2,1)S(1)}, bf16[256,1024]{1,0:T(8,128)(2,1)}, u32[]{:S(2)}) copy-start(bf16[256,1024]{1,0:T(8,128)(2,1)} %get-tuple-element.13) | copy-start | bytes 1572868
  59.6 6.2 %copy-start = (bf16[256,1024]{1,0:T(8,128)(2,1)S(1)}, bf16[256,1024]{1,0:T(8,128)(2,1)}, u32[]{:S(2)}) copy-start(bf16[256,1024]{1,0:T(8,128)(2,1)} %get-tuple-element.14) | copy-start | bytes 1572868

commit v3 on v2

--- a/solution.py
+++ b/solution.py
@@ -340,15 +340,15 @@
             inv_ref[u] = inv
             wt_ref[u] = f * inv
 
-    def in_twos(step, first, stop):
+    def in_twos(step, first, stop, together=2):
         def body(i, carry):
-            step(2 * i)
-            step(2 * i + 1)
+            for j in range(together):
+                step(together * i + j)
             return carry
 
-        lax.fori_loop(first // 2, stop // 2, body, 0)
-
-    in_twos(forward, 0, pairs)
+        lax.fori_loop(first // together, stop // together, body, 0)
+
+    in_twos(forward, 0, pairs, 4)
 
     start_first()
     mixed_ref[...] = dot(att_ref[...], w_ref[...]).astype(BF16)

time: 66.8 us -> 66.3 us (level)
  no operation moved by 1% of the time
where the time goes in v3:
time: 66.3 us; the launch traced here: 66.1 us
  Pallas kernels  58.4 us (88%)
  local copies, waits for them, and re-layouts  6.98 us (11%)
    pallas_call x1, Pallas kernels, on_device(): pl.pallas_call(functools.partial(kernel, n, span_one, span_two), out_shap...  58.4 us
    unnamed x9, local copies, waits for them, and re-layouts  6.98 us

profile of v3, /device:TPU:0, one launch (start us, length us, event | category | flops | bytes accessed | tf_op | source)
XLA Modules:
  0.0 66.1 jit_solution(13638978021288786400)
XLA Ops:
  0.6 58.4 %shard_map.92 = (bf16[256,1024]{1,0:T(8,128)(2,1)}, f32[32,1024]{1,0:T(8,128)}, bf16[256,1024]{1,0:T(8,128)(2,1)}, bf16[256,1024]{1,0:T(8,128)(2,1)}, bf16[256,1024]{1,0:T(8,128)(2,1)}) custom-call(bf16[256,1024]{1,0:T(8,128)(2,1)} %bitcast.12, bf16[256,1024]{1,0:T(8,128)(2,1)} %bitcast.13, bf16[256,1024]{1,0:T(8,128)(2,1)} %bitcast.14, ...), custom_call_target="tpu_custom_call" | custom-call | tf_op jit(solution)/shard_map/pallas_call | solution.py:496
  59.1 0.0 copy-start.1
  59.1 0.0 copy-start
  59.1 2.0 %copy.15 = bf16[1,256,1024]{2,1,0:T(8,128)(2,1)} copy(bf16[1,256,1024]{2,1,0:T(8,128)(2,1)} %bitcast.11) | data formatting | bytes 1048576
  61.0 1.6 %copy.16 = f32[32,1024]{1,0:T(8,128)} copy(f32[32,1024]{1,0:T(8,128)} %get-tuple-element.21) | data formatting | bytes 262144
  62.6 1.9 %copy.17 = bf16[1,256,1024]{2,1,0:T(8,128)(2,1)} copy(bf16[1,256,1024]{2,1,0:T(8,128)(2,1)} %bitcast.10) | data formatting | bytes 1048576
  64.5 0.0 copy-done.1
  64.5 0.8 %copy.18 = bf16[1,256,1024]{2,1,0:T(8,128)(2,1)} copy(bf16[1,256,1024]{2,1,0:T(8,128)(2,1)S(1)} %bitcast.9) | data formatting | bytes 1048576
  65.3 0.0 copy-done
  65.3 0.8 %copy.19 = bf16[1,256,1024]{2,1,0:T(8,128)(2,1)} copy(bf16[1,256,1024]{2,1,0:T(8,128)(2,1)S(1)} %bitcast.8) | data formatting | bytes 1048576
Async XLA Ops:
  59.1 5.4 %copy-start.1 = (bf16[256,1024]{1,0:T(8,128)(2,1)S(1)}, bf16[256,1024]{1,0:T(8,128)(2,1)}, u32[]{:S(2)}) copy-start(bf16[256,1024]{1,0:T(8,128)(2,1)} %get-tuple-element.13) | copy-start | bytes 1572868
  59.1 6.2 %copy-start = (bf16[256,1024]{1,0:T(8,128)(2,1)S(1)}, bf16[256,1024]{1,0:T(8,128)(2,1)}, u32[]{:S(2)}) copy-start(bf16[256,1024]{1,0:T(8,128)(2,1)} %get-tuple-element.14) | copy-start | bytes 1572868

commit v4 on v3

--- a/solution.py
+++ b/solution.py
@@ -184,6 +184,16 @@
         remote(v_ref.at[top], vext.at[bottom], halo_send.at[3], halo_recv.at[3], left),
     ]
 
+    @pl.when(has_right)
+    def _():
+        for copy in to_right:
+            copy.start()
+
+    @pl.when(has_left)
+    def _():
+        for copy in to_left:
+            copy.start()
+
     r_id, i_id = iota((SLOT, rows), 0), iota((SLOT, rows), 1)
 
     def pick(rid):
@@ -212,16 +222,6 @@
     for o in range(1, n):
         peer = lax.rem(me + o, n)
         remote(pool.at[me], pool.at[me], pool_send.at[o], pool_recv.at[o], peer).start()
-
-    @pl.when(has_right)
-    def _():
-        for copy in to_right:
-            copy.start()
-
-    @pl.when(has_left)
-    def _():
-        for copy in to_left:
-            copy.start()
 
     kext[BLOCK : BLOCK + rows] = k_ref[...]
     vext[BLOCK : BLOCK + rows] = v_ref[...]

time: 66.3 us -> 66.8 us (level)
  no operation moved by 1% of the time
where the time goes in v4:
time: 66.8 us; the launch traced here: 66.6 us
  Pallas kernels  59 us (88%)
  local copies, waits for them, and re-layouts  6.98 us (10%)
    pallas_call x1, Pallas kernels, on_device(): pl.pallas_call(functools.partial(kernel, n, span_one, span_two), out_shap...  59 us
    unnamed x9, local copies, waits for them, and re-layouts  6.98 us

profile of v4, /device:TPU:0, one launch (start us, length us, event | category | flops | bytes accessed | tf_op | source)
XLA Modules:
  0.0 66.6 jit_solution(8478334592473693599)
XLA Ops:
  0.6 59.0 %shard_map.92 = (bf16[256,1024]{1,0:T(8,128)(2,1)}, f32[32,1024]{1,0:T(8,128)}, bf16[256,1024]{1,0:T(8,128)(2,1)}, bf16[256,1024]{1,0:T(8,128)(2,1)}, bf16[256,1024]{1,0:T(8,128)(2,1)}) custom-call(bf16[256,1024]{1,0:T(8,128)(2,1)} %bitcast.12, bf16[256,1024]{1,0:T(8,128)(2,1)} %bitcast.13, bf16[256,1024]{1,0:T(8,128)(2,1)} %bitcast.14, ...), custom_call_target="tpu_custom_call" | custom-call | tf_op jit(solution)/shard_map/pallas_call | solution.py:496
  59.6 0.0 copy-start.1
  59.6 0.0 copy-start
  59.6 2.0 %copy.15 = bf16[1,256,1024]{2,1,0:T(8,128)(2,1)} copy(bf16[1,256,1024]{2,1,0:T(8,128)(2,1)} %bitcast.11) | data formatting | bytes 1048576
  61.6 1.6 %copy.16 = f32[32,1024]{1,0:T(8,128)} copy(f32[32,1024]{1,0:T(8,128)} %get-tuple-element.21) | data formatting | bytes 262144
  63.1 1.9 %copy.17 = bf16[1,256,1024]{2,1,0:T(8,128)(2,1)} copy(bf16[1,256,1024]{2,1,0:T(8,128)(2,1)} %bitcast.10) | data formatting | bytes 1048576
  65.0 0.0 copy-done.1
  65.0 0.8 %copy.18 = bf16[1,256,1024]{2,1,0:T(8,128)(2,1)} copy(bf16[1,256,1024]{2,1,0:T(8,128)(2,1)S(1)} %bitcast.9) | data formatting | bytes 1048576
  65.8 0.0 copy-done
  65.8 0.8 %copy.19 = bf16[1,256,1024]{2,1,0:T(8,128)(2,1)} copy(bf16[1,256,1024]{2,1,0:T(8,128)(2,1)S(1)} %bitcast.8) | data formatting | bytes 1048576
Async XLA Ops:
  59.6 5.4 %copy-start.1 = (bf16[256,1024]{1,0:T(8,128)(2,1)S(1)}, bf16[256,1024]{1,0:T(8,128)(2,1)}, u32[]{:S(2)}) copy-start(bf16[256,1024]{1,0:T(8,128)(2,1)} %get-tuple-element.13) | copy-start | bytes 1572868
  59.6 6.2 %copy-start = (bf16[256,1024]{1,0:T(8,128)(2,1)S(1)}, bf16[256,1024]{1,0:T(8,128)(2,1)}, u32[]{:S(2)}) copy-start(bf16[256,1024]{1,0:T(8,128)(2,1)} %get-tuple-element.14) | copy-start | bytes 1572868
